TPU v7x, 512 devices: a whole 4x4x16 slice. The times are simulated.
512 devices in a mesh: row: 32 (over y, x, core), col: 16 (over z).
Axes of the slice: x: 4, y: 4, z: 16, core: 2. Of those that a mesh axis runs over, the one named last changes fastest.
Arguments:
- points: float32 [65536, 128], P(('row', 'col')), may hold values from -6 to 6
- lengthscales: float32 [128], replicated, may hold values from 3.0547013 to 5.9962654
- noise: float32 [65536], P(('row', 'col')), may hold values from 0.5 to 2
- targets: float32 [32, 65536], P(None, ('row', 'col')), may hold values from -6 to 6
Outputs:
- solution: float32 [32, 65536], P(None, ('row', 'col'))
- residual: float32 [32, 65536], P(None, ('row', 'col'))
- direction: float32 [32, 65536], P(None, ('row', 'col'))
All inputs are finite; a program needn't handle non-finite values.
Results may differ from a plain program's by a relative error of at most 0.0077.
Values may be sent and summed in bfloat16 or wider, within the bound.
A program may use at most 64 MiB of HBM per device.

v0:
```python
import math

import jax
import jax.numpy as jnp
from jax import lax
from jax.sharding import PartitionSpec as P

root_five = 5.0**0.5


def chol_solve(matrix, rhs):
    return jax.scipy.linalg.cho_solve((jnp.linalg.cholesky(matrix), True), rhs)


def matern(left, left_sq, right, right_sq):
    cross = jnp.dot(left, right.T, preferred_element_type=jnp.float32)
    dist_sq = jnp.maximum(left_sq[:, None] + right_sq[None, :] - 2.0 * cross, 0.0)
    dist = jnp.sqrt(dist_sq)
    value = (1.0 + root_five * dist + 5.0 / 3.0 * dist_sq) * jnp.exp(-root_five * dist)
    return value.astype(jnp.bfloat16)


def squares(values):
    return jnp.sum(jnp.square(values.astype(jnp.float32)), axis=1)


def make_fold(local_rows, carry, piece):
    local_sq = squares(local_rows)
    count = local_rows.shape[0]
    block_rows = math.gcd(count, 512)
    far_points, far_dirs = piece
    far_sq = squares(far_points)

    def advance(index, total):
        begin = index * block_rows
        rows = lax.dynamic_slice_in_dim(local_rows, begin, block_rows, 0)
        rows_sq = lax.dynamic_slice_in_dim(local_sq, begin, block_rows, 0)
        tile = matern(rows, rows_sq, far_points, far_sq)
        term = lax.dot_general(
            far_dirs, tile, (((0,), (1,)), ((), ())), preferred_element_type=jnp.float32
        )
        before = lax.dynamic_slice_in_dim(total, begin, block_rows, 1)
        return lax.dynamic_update_slice_in_dim(total, before + term, begin, 1)

    return lax.fori_loop(0, count // block_rows, advance, carry)


def gram(left, right):
    return jnp.dot(left, right.T, precision=lax.Precision.HIGHEST)


def per_device(points, lengthscales, noise, targets):
    precise = lax.Precision.HIGHEST
    scaled = (points / lengthscales[None, :]).astype(jnp.bfloat16)
    dir_rows = targets.T.astype(jnp.bfloat16)
    quantiles = targets.shape[0]
    local_rows = lax.all_gather(scaled, "col", axis=0, tiled=True)
    empty = jnp.zeros((quantiles, local_rows.shape[0]), jnp.float32)
    partial_sum = make_fold(
        local_rows,
        empty,
        (
            lax.all_gather(scaled, "row", axis=0, tiled=True),
            lax.all_gather(dir_rows, "row", axis=0, tiled=True),
        ),
    )
    product = lax.psum_scatter(partial_sum, "col", scatter_dimension=1, tiled=True)
    image = product + noise[None, :] * targets
    first = lax.psum(gram(targets, targets), ("row", "col"))
    curvature = lax.psum(gram(targets, image), ("row", "col"))
    step_matrix = chol_solve(curvature, first)
    residual = targets - jnp.dot(step_matrix.T, image, precision=precise)
    norm_new = lax.psum(gram(residual, residual), ("row", "col"))
    solution = jnp.dot(step_matrix.T, targets, precision=precise)
    ratio = chol_solve(first, norm_new)
    direction = residual + jnp.dot(ratio.T, targets, precision=precise)
    return (solution, residual, direction)


def solution(mesh):
    return jax.shard_map(
        per_device,
        mesh=mesh,
        in_specs=(P(("row", "col"), None), P(), P(("row", "col")), P(None, ("row", "col"))),
        out_specs=(P(None, ("row", "col")), P(None, ("row", "col")), P(None, ("row", "col"))),
        check_vma=False,
    )
```

profile of v0, /device:TPU:1, one launch (start us, length us, event | category | flops | bytes accessed | tf_op | source)
XLA Modules:
  0.0 395.4 jit_solution(6089042122263511336)
XLA Ops:
  7.2 0.0 all-gather.2.cloned.1.call-start
  7.2 1.5 divide_convert_fusion
  8.7 0.0 copy-start.3
  8.7 0.0 all-gather.2.cloned.1.call-update
  8.7 0.0 reduce-scatter.2.cloned.1.call-start
  8.7 0.7 convert_bitcast_fusion
  9.5 28.2 %all_gather.11 = bf16[4096,32]{0,1:T(8,128)(2,1)S(1)} all-gather(bf16[128,32]{0,1:T(8,128)(2,1)S(1)} %convert_bitcast_fusion), channel_id=1, replica_groups=mesh['row'=32,'col'=16] {'row'}, dimensions={0}, use_global_device_ids=true | all-gather | bytes 270336 | tf_op jit(solution)/shard_map/all_gather | solution.py:64
  37.7 0.5 copy.11
  38.2 0.0 copy-done.3
  38.2 29.3 %all_gather.9 = bf16[2048,128]{1,0:T(8,128)(2,1)S(1)} all-gather(bf16[128,128]{1,0:T(8,128)(2,1)S(1)} %copy-done.3), channel_id=1, replica_groups=mesh['row'=32,'col'=16] {'col'}, dimensions={0}, use_global_device_ids=true | all-gather | bytes 557056 | tf_op jit(solution)/shard_map/all_gather | solution.py:57
  67.5 0.3 multiply_reduce_fusion.1
  67.9 7.1 %all-gather.2.cloned.1.call-done = bf16[4096,128]{1,0:T(8,128)(2,1)} async-done(((bf16[128,128]{1,0:T(8,128)(2,1)}), bf16[4096,128]{1,0:T(8,128)(2,1)}) %all-gather.2.cloned.1.call-update) | async-done | bytes 1048592 | tf_op jit(solution)/shard_map/all_gather | solution.py:63
  75.0 0.0 copy-start
  75.0 1.9 multiply_reduce_fusion
  77.0 0.0 copy-done
  77.0 0.0 copy-start.2
  77.0 0.0 copy-start.5
  77.0 23.4 %while.13 = (s32[]{:T(128)}, f32[32,2048]{1,0:T(8,128)S(1)}, f32[2048]{0:T(1024)S(1)}, f32[4096]{0:T(1024)S(1)}, bf16[2048,128]{1,0:T(8,128)(2,1)S(1)}, /*index=...) while((s32[]{:T(128)}, f32[32,2048]{1,0:T(8,128)S(1)}, ...), condition=%wide.region_3.0_spmd, body=%wide.region_2.0_spmd.sunk | while | flops 694173696 | bytes 2383007 | solution.py:45
  77.0 0.1 dynamic_slice.30
  77.1 5.8 %fusion.54 = f32[32,2048]{1,0:T(8,128)S(1)} fusion(f32[32,2048]{1,0:T(8,128)S(1)} %get-tuple-element.210, s32[]{:T(128)S(6)} %select_n.23, bf16[4096,32]{1,0:T(8,128)(2,1)S(1)} %get-tuple-element.226, bf16[4096,128]{1,0:T(8,128)(2,1)S(1)} %get-tuple-element.225, f32[4096]{0:T(1024)S(1)} %get-tuple-element.223, f32[512]{0:T(512)S(1)} %dynamic_slice.30, ...), kind=kOutput, calls=%fused_computation.4.clone.1 | convolution fusion | flops 694173696 | bytes 2378752 | tf_op jit(solution)/shard_map/while/body/eval_jaxpr/dot_general | solution.py:39
  82.9 0.1 dynamic_slice.30
  83.0 5.8 %fusion.54 = f32[32,2048]{1,0:T(8,128)S(1)} fusion(f32[32,2048]{1,0:T(8,128)S(1)} %get-tuple-element.210, s32[]{:T(128)S(6)} %select_n.23, bf16[4096,32]{1,0:T(8,128)(2,1)S(1)} %get-tuple-element.226, bf16[4096,128]{1,0:T(8,128)(2,1)S(1)} %get-tuple-element.225, f32[4096]{0:T(1024)S(1)} %get-tuple-element.223, f32[512]{0:T(512)S(1)} %dynamic_slice.30, ...), kind=kOutput, calls=%fused_computation.4.clone.1 | convolution fusion | flops 694173696 | bytes 2378752 | tf_op jit(solution)/shard_map/while/body/eval_jaxpr/dot_general | solution.py:39
  88.8 0.1 dynamic_slice.30
  88.8 5.8 %fusion.54 = f32[32,2048]{1,0:T(8,128)S(1)} fusion(f32[32,2048]{1,0:T(8,128)S(1)} %get-tuple-element.210, s32[]{:T(128)S(6)} %select_n.23, bf16[4096,32]{1,0:T(8,128)(2,1)S(1)} %get-tuple-element.226, bf16[4096,128]{1,0:T(8,128)(2,1)S(1)} %get-tuple-element.225, f32[4096]{0:T(1024)S(1)} %get-tuple-element.223, f32[512]{0:T(512)S(1)} %dynamic_slice.30, ...), kind=kOutput, calls=%fused_computation.4.clone.1 | convolution fusion | flops 694173696 | bytes 2378752 | tf_op jit(solution)/shard_map/while/body/eval_jaxpr/dot_general | solution.py:39
  94.6 0.1 dynamic_slice.30
  94.7 5.8 %fusion.54 = f32[32,2048]{1,0:T(8,128)S(1)} fusion(f32[32,2048]{1,0:T(8,128)S(1)} %get-tuple-element.210, s32[]{:T(128)S(6)} %select_n.23, bf16[4096,32]{1,0:T(8,128)(2,1)S(1)} %get-tuple-element.226, bf16[4096,128]{1,0:T(8,128)(2,1)S(1)} %get-tuple-element.225, f32[4096]{0:T(1024)S(1)} %get-tuple-element.223, f32[512]{0:T(512)S(1)} %dynamic_slice.30, ...), kind=kOutput, calls=%fused_computation.4.clone.1 | convolution fusion | flops 694173696 | bytes 2378752 | tf_op jit(solution)/shard_map/while/body/eval_jaxpr/dot_general | solution.py:39
  100.5 0.0 copy-start.1
  100.5 0.7 copy-done.1
  101.2 0.0 reduce-scatter.2.cloned.1.call-update
  101.2 0.0 copy-done.2
  101.2 0.1 fusion.28
  101.3 56.3 %reduce-scatter.2.cloned.1.call-done = f32[32,128]{1,0:T(8,128)} async-done(((f32[32,2048]{1,0:T(8,128)}), f32[32,128]{1,0:T(8,128)}) %reduce-scatter.2.cloned.1.call-update) | async-done | bytes 16400 | tf_op jit(solution)/shard_map/reduce_scatter | solution.py:67
  157.6 0.0 copy-done.5
  157.6 0.9 convolution_bitcast_fusion
  158.5 112.8 %all-reduce = (f32[32,32]{0,1:T(8,128)S(1)}, f32[32,32]{0,1:T(8,128)S(1)}) all-reduce(f32[32,32]{0,1:T(8,128)S(1)} %fusion.28, f32[32,32]{0,1:T(8,128)S(1)} %convolution_bitcast_fusion), channel_id=1, replica_groups=mesh['row'=32,'col'=16] {'row','col'}, use_global_device_ids=true, to_apply=%region_8.10 | all-reduce | flops 2048 | bytes 16384 | tf_op jit(solution)/shard_map/psum | solution.py:69
  271.3 0.1 copy.14
  271.4 0.1 copy.12
  271.5 2.9 cholesky.55
  274.4 0.6 compare_reduce_fusion
  275.0 0.7 fusion.15
  275.7 2.4 custom-call.9
  278.1 2.9 cholesky.44
  281.1 0.6 compare_reduce_fusion.1
  281.8 0.7 fusion.14
  282.4 2.4 custom-call.8
  284.8 0.2 fusion.23
  285.1 0.1 fusion.21
  285.2 0.8 fusion.29
  286.1 0.9 convolution_subtract_fusion
  287.0 0.0 copy-start.4
  287.0 0.1 fusion.30
  287.2 100.2 %psum.23 = f32[32,32]{1,0:T(8,128)S(1)} all-reduce(f32[32,32]{1,0:T(8,128)S(1)} %fusion.30), channel_id=1, replica_groups=mesh['row'=32,'col'=16] {'row','col'}, use_global_device_ids=true, to_apply=%region_9.12 | all-reduce | flops 1024 | bytes 8192 | tf_op jit(solution)/shard_map/psum | solution.py:73
  387.3 0.2 fusion.18
  387.5 0.1 fusion.16
  387.7 0.8 convolution_add_fusion
  388.5 0.0 copy-done.4
  (4 shorter events, 0.1 us)
Async XLA Ops:
  7.2 67.8 %all-gather.2.cloned.1.call-start = ((), (), s32[]{:S(2)}) async-start(), calls=%async_computation.1 | async-start | bytes 1081344 | tf_op jit(solution)/shard_map/all_gather | solution.py:63
  8.7 29.5 %copy-start.3 = (bf16[128,128]{1,0:T(8,128)(2,1)S(1)}, bf16[128,128]{1,0:T(8,128)(2,1)}, u32[]{:S(2)}) copy-start(bf16[128,128]{1,0:T(8,128)(2,1)} %divide_convert_fusion) | copy-start | bytes 98308
  8.7 148.9 %reduce-scatter.2.cloned.1.call-start = ((), (), s32[]{:S(2)}) async-start(), calls=%async_computation.2 | async-start | bytes 278528 | tf_op jit(solution)/shard_map/reduce_scatter | solution.py:67
  75.0 2.0 copy-start
  77.0 24.2 %copy-start.2 = (f32[32,128]{1,0:T(8,128)S(1)}, f32[32,128]{1,0:T(8,128)}, u32[]{:S(2)}) copy-start(f32[32,128]{1,0:T(8,128)} %param.12) | copy-start | bytes 49156
  77.0 80.6 %copy-start.5 = (f32[128]{0:T(128)S(1)}, f32[128]{0:T(128)}, u32[]{:S(2)}) copy-start(f32[128]{0:T(128)} %param.11) | copy-start | bytes 1540
  100.5 0.7 copy-start.1
  287.0 101.5 %copy-start.4 = (f32[32,128]{1,0:T(8,128)}, f32[32,128]{1,0:T(8,128)S(1)}, u32[]{:S(2)}) copy-start(f32[32,128]{1,0:T(8,128)S(1)} %convolution_subtract_fusion) | copy-start | bytes 49156
Sparse Core Ops, SparseCore 0:
  11.1 63.8 all-gather.1
  101.3 56.2 reduce-scatter.1
where the time goes:
time: 396 us; the launch traced here: 395 us
  blocking collectives  271 us (68%)
  waiting for transfers between devices  63.4 us (16%)
  matrix products  27.5 us (7%)
  other arithmetic  17.8 us (4%)
  between operations  14.2 us (4%)
    psum x1, blocking collectives, per_device(): first = lax.psum(gram(targets, targets), ('row', 'col'))  113 us
    psum x1, blocking collectives, per_device(): norm_new = lax.psum(gram(residual, residual), ('row', 'col'))  100 us
    reduce_scatter x1, waiting for transfers between devices, per_device(): lax.psum_scatter(partial_sum, 'col', scatter_dimension=1, tiled=True)  56.3 us
    all_gather x1, blocking collectives, per_device(): local_rows = lax.all_gather(scaled, 'col', axis=0, tiled=True)  29.3 us
    all_gather x1, blocking collectives, per_device(): lax.all_gather(dir_rows, 'row', axis=0, tiled=True)  28.2 us
    dot_general x4, matrix products, advance(): lax.dot_general(far_dirs, tile, (((0,), (1,)), ((), ())), preferred_eleme...  23 us
    another operation x10, other arithmetic, chol_solve(): return jax.scipy.linalg.cho_solve((jnp.linalg.cholesky(matrix), True), rhs)  13.4 us
  transfers between devices with their start and end apart: 2, of which 2 were waited for; matrix products, arithmetic and copies ran while one was open for 0% of the time, Pallas kernels for 0%

commit v1 on v0

v1 whole, which is shorter than its diff:
```python
import functools

import jax
import jax.numpy as jnp
from jax import lax
from jax.experimental import pallas as pl
from jax.experimental.pallas import tpu as pltpu
from jax.sharding import PartitionSpec as P

MESH = pl.DeviceIdType.MESH
HI = lax.Precision.HIGHEST
root_five = 5.0**0.5
log2_e = 1.4426950408889634

PLANE = 16
RING = 16
BLOCK = 128
RHS = 32
DIRECT = (6, -6, 3, -3, 1, -1)
NEAR = (0,) + DIRECT
FAR = (2, -2, 4, -4, 5, -5, 7, -7, 8)
OFFSETS = NEAR + FAR
FORWARD = {6: (1, -1, 2), -6: (1, -1), 3: (1, -1), -3: (1, -1), 1: (), -1: ()}
PAIR = 2 * BLOCK


def place():
    row, col = lax.axis_index("row"), lax.axis_index("col")
    return lax.div(row, 8), lax.rem(lax.div(row, 2), 4), lax.rem(row, 2), col


def in_plane(step):
    y, x, core, z = place()
    y = lax.rem(y + lax.div(step, 4), 4)
    x = lax.rem(x + lax.rem(step, 4), 4)
    return (y * 8 + x * 2 + core, z)


def back(step):
    return lax.rem(4 - lax.div(step, 4), 4) * 4 + lax.rem(4 - lax.rem(step, 4), 4)


def along_z(step):
    y, x, core, z = place()
    return (y * 8 + x * 2 + core, lax.rem(z + (step + RING), RING))


def other_core():
    y, x, core, z = place()
    return (y * 8 + x * 2 + 1 - core, z)


def remote(src, dst, send, recv, device):
    return pltpu.make_async_remote_copy(
        src_ref=src, dst_ref=dst, send_sem=send, recv_sem=recv, device_id=device, device_id_type=MESH
    )


def landed(ref, sem):
    pltpu.make_async_copy(ref, ref, sem).wait()


def split_norms(rows):
    wide = rows.astype(jnp.float32)
    norm = jnp.sum(wide * wide, axis=1, keepdims=True)
    high = norm.astype(jnp.bfloat16).astype(jnp.float32)
    rest = norm - high
    middle = rest.astype(jnp.bfloat16).astype(jnp.float32)
    return high, middle, rest - middle


def norm_lanes(rows, first):
    high, middle, low = split_norms(rows)
    lane = lax.broadcasted_iota(jnp.int32, rows.shape, 1)
    ones = 3 - first
    value = jnp.where((lane >= ones) & (lane < ones + 3), 1.0, 0.0)
    value = jnp.where(lane == first, high, value)
    value = jnp.where(lane == first + 1, middle, value)
    return jnp.where(lane == first + 2, low, value).astype(jnp.bfloat16)


def matern(dist_sq):
    dist_sq = jnp.maximum(dist_sq, 1e-30)
    dist = dist_sq * lax.rsqrt(dist_sq)
    decay = jnp.exp2(dist * (-root_five * log2_e))
    return (((5.0 / 3.0 * dist_sq + 1.0) + root_five * dist) * decay).astype(jnp.bfloat16)


def product(dirs, rows, norms, out_points):
    dist_sq = lax.dot_general(
        jnp.concatenate([rows, norms], axis=1), out_points, (((1,), (1,)), ((), ())), preferred_element_type=jnp.float32
    )
    return jnp.dot(dirs, matern(dist_sq), preferred_element_type=jnp.float32)


def eliminate(matrix):
    row = lax.broadcasted_iota(jnp.int32, matrix.shape, 0)
    for k in range(RHS):
        pivot = matrix[k : k + 1, :] / matrix[k : k + 1, k : k + 1]
        matrix = jnp.where(row == k, pivot, matrix - matrix[:, k : k + 1] * pivot)
    return matrix


def shift(value, lanes):
    return pltpu.roll(value, lanes % 128, 1)


def precise(left, right):
    return jnp.dot(left, right, precision=HI, preferred_element_type=jnp.float32)


def gram(left, right):
    return lax.dot_general(left, right, (((1,), (1,)), ((), ())), precision=HI, preferred_element_type=jnp.float32)


def pack(rows):
    lane = lax.broadcasted_iota(jnp.int32, (8, 128), 1)
    return jnp.where(lane < 64, rows[0:8], shift(rows[8:16], 64))


def wide(value):
    return jnp.concatenate([value, jnp.zeros((value.shape[0], 128 - value.shape[1]), value.dtype)], axis=1)


class Sum:
    def __init__(self, parts, plane, ring, halves, sems):
        self.parts, self.plane, self.ring, self.halves = parts, plane, ring, halves
        self.core_send, self.core_recv, self.plane_send, self.plane_recv, self.ring_send, self.ring_recv = sems

    def begin(self, value):
        core = place()[2]
        first, second = pack(value[0:16]), pack(value[16:32])
        low = core == 0
        self.parts[0] = jnp.where(low, first, second)
        self.parts[1] = jnp.where(low, second, first)
        remote(self.parts.at[1], self.parts.at[2], self.core_send.at[0], self.core_recv.at[0], other_core()).start()

    def over_plane(self):
        y, x, _, _ = place()
        me = y * 4 + x
        landed(self.parts.at[2], self.core_recv.at[0])
        self.plane[me] = self.parts[0] + self.parts[2]

        def send(k, _):
            remote(self.plane.at[me], self.plane.at[me], self.plane_send.at[k], self.plane_recv, in_plane(k)).start()
            return 0

        lax.fori_loop(1, PLANE, send, 0, unroll=True)

    def over_ring(self):
        me = place()[3]
        landed(self.plane.at[pl.ds(1, PLANE - 1)], self.plane_recv)
        self.ring[me] = jnp.sum(self.plane[...], axis=0)
        for k in (8, -7, 7, -6, 6, -5, 5, -4, 4, -3, 3, -2, 2, -1, 1):
            remote(self.ring.at[me], self.ring.at[me], self.ring_send.at[k % RING], self.ring_recv, along_z(k)).start()

    def over_cores(self):
        core = place()[2]
        landed(self.ring.at[pl.ds(1, RING - 1)], self.ring_recv)
        self.halves[core] = jnp.sum(self.ring[...], axis=0)
        remote(self.halves.at[core], self.halves.at[core], self.core_send.at[1], self.core_recv.at[1], other_core()).start()

    def end(self):
        landed(self.halves.at[0], self.core_recv.at[1])
        first, second = self.halves[0], self.halves[1]
        return jnp.concatenate([first, shift(first, 64), second, shift(second, 64)], axis=0)

    def sent(self):
        landed(self.parts.at[1], self.core_send.at[0])
        landed(self.halves.at[0], self.core_send.at[1])
        for k in range(1, PLANE):
            landed(self.plane.at[0], self.plane_send.at[k])
        for k in range(1, RING):
            landed(self.ring.at[0], self.ring_send.at[k])


def kernel(
    points, scales, noise, targets, solution_ref, residual_ref, direction_ref,
    near_far, norms, out_raw, out_points, own, total, outbox, inbox,
    parts_a, plane_a, ring_a, halves_a, parts_b, plane_b, ring_b, halves_b,
    in_send, in_recv, across_send, across_recv, forward_send, out_send, out_recv, box_send, box_recv,
    cs_a, cr_a, ps_a, pr_a, rs_a, rr_a, cs_b, cr_b, ps_b, pr_b, rs_b, rr_b,
):
    barrier = pltpu.get_barrier_semaphore()

    def greet(device):
        pl.semaphore_signal(barrier, inc=1, device_id=device, device_id_type=MESH)

    def greet_plane(k, _):
        greet(in_plane(k))
        return 0

    for k in (8, -7, 7, -6, 6, -5, 5, -4, 4, -3, 3, -2, 2, -1, 1):
        greet(along_z(k))
    lax.fori_loop(1, PLANE, greet_plane, 0, unroll=True)
    greet(other_core())

    goals = targets[...]
    scaled = (points[...] / scales[...]).astype(jnp.bfloat16)
    own[...] = scaled
    near_far[0, 0:BLOCK] = scaled
    near_far[0, BLOCK : BLOCK + RHS] = goals.astype(jnp.bfloat16)
    norms[0:BLOCK] = norm_lanes(scaled, 0)
    out_points[15 * BLOCK : 16 * BLOCK, 0:BLOCK] = scaled * -2.0
    out_points[15 * BLOCK : 16 * BLOCK, BLOCK:PAIR] = norm_lanes(scaled, 3)
    first_sum = Sum(parts_a, plane_a, ring_a, halves_a, (cs_a, cr_a, ps_a, pr_a, rs_a, rr_a))
    last_sum = Sum(parts_b, plane_b, ring_b, halves_b, (cs_b, cr_b, ps_b, pr_b, rs_b, rr_b))
    first_part = wide(gram(goals, goals))

    pl.semaphore_wait(barrier, (RING - 1) + (PLANE - 1) + 1)

    for i, step in enumerate(OFFSETS):
        if step in DIRECT:
            remote(near_far.at[0], near_far.at[2 * i], in_send.at[i], in_recv.at[i], along_z(step)).start()

    def across(i):
        remote(near_far.at[2 * i], near_far.at[2 * i + 1], across_send.at[i], across_recv.at[i], other_core()).start()

    def send_out(k, _):
        slot = 15 - back(k)
        remote(own, out_raw.at[slot], out_send.at[k], out_recv.at[slot], in_plane(k)).start()
        return 0

    lax.fori_loop(1, PLANE, send_out, 0, unroll=True)
    across(0)
    first_sum.begin(first_part)

    def arrived(i):
        landed(near_far.at[2 * i], in_recv.at[i])
        across(i)

    def take(slot):
        norms[slot * BLOCK : (slot + 1) * BLOCK] = norm_lanes(near_far[slot, 0:BLOCK], 0)

    forwards = []
    for step in (1, -1, 3, -3, 6, -6):
        i = OFFSETS.index(step)
        arrived(i)
        for more in FORWARD[step]:
            j = OFFSETS.index(step + more)
            n = len(forwards)
            forwards.append(j)
            remote(near_far.at[2 * i], near_far.at[2 * j], forward_send.at[n], in_recv.at[j], along_z(more)).start()
        take(2 * i)
    first_sum.over_plane()

    def take_out(slot, _):
        landed(out_raw.at[slot], out_recv.at[slot])
        rows = out_raw[slot]
        at = pl.ds(pl.multiple_of(slot * BLOCK, BLOCK), BLOCK)
        out_points[at, 0:BLOCK] = rows * -2.0
        out_points[at, BLOCK:PAIR] = norm_lanes(rows, 3)
        return 0

    lax.fori_loop(0, PLANE - 1, take_out, 0)

    def take_across(i):
        landed(near_far.at[2 * i + 1], across_recv.at[i])
        take(2 * i + 1)

    for i in range(len(NEAR)):
        take_across(i)

    def partial(begin, end, o):
        rows = near_far[begin:end, 0:BLOCK].reshape((end - begin) * BLOCK, BLOCK)
        dirs = jnp.concatenate([near_far[s, BLOCK : BLOCK + RHS] for s in range(begin, end)], axis=1)
        at = pl.ds(pl.multiple_of(o * PAIR, PAIR), PAIR)
        return product(dirs, rows, norms[begin * BLOCK : end * BLOCK], out_points[at, :])

    near_slots, slots = 2 * len(NEAR), 2 * len(OFFSETS)

    def near_part(o, _):
        total[o] = partial(0, near_slots, o)
        return 0

    lax.fori_loop(0, PLANE // 2, near_part, 0)

    for i in range(len(NEAR), len(OFFSETS)):
        arrived(i)
        take(2 * i)
    first_sum.over_ring()
    for i in range(len(NEAR), len(OFFSETS)):
        take_across(i)

    def far_part(o, _):
        value = total[o] + partial(near_slots, slots, o)
        outbox[2 * o] = value[:, 0:BLOCK]
        outbox[2 * o + 1] = value[:, BLOCK:PAIR]

        def post(slot):
            step = 15 - slot
            remote(outbox.at[slot], inbox.at[slot], box_send.at[slot], box_recv, in_plane(step)).start()

        post(2 * o)

        @pl.when(o < PLANE // 2 - 1)
        def _():
            post(2 * o + 1)

        return 0

    lax.fori_loop(0, PLANE // 2, far_part, 0)
    first_sum.over_cores()

    lane = lax.broadcasted_iota(jnp.int32, (RHS, 128), 1)
    row = lax.broadcasted_iota(jnp.int32, (RHS, 128), 0)
    first = jnp.where(lane < RHS, first_sum.end(), 0.0)
    identity = jnp.where(lane == row + RHS, 1.0, 0.0)
    first_inverse = shift(eliminate(first + identity), -RHS)[:, 0:RHS]

    landed(inbox.at[pl.ds(0, PLANE - 1)], box_recv)
    image = (jnp.sum(inbox[0 : PLANE - 1], axis=0) + outbox[PLANE - 1]) + noise[...] * goals

    last_sum.begin(wide(gram(image, jnp.concatenate([goals, image], axis=0))))
    last_sum.over_plane()
    last_sum.over_ring()
    last_sum.over_cores()
    sums = last_sum.end()
    turned = sums[:, 0:RHS]
    curvature = wide(0.5 * (turned + turned.T))
    solved = eliminate(curvature + shift(first, RHS))
    step_matrix = shift(solved, -RHS)[:, 0:RHS]
    step_turned = step_matrix.T
    moved = precise(step_turned, jnp.concatenate([goals, image], axis=1))
    residual = goals - moved[:, 128:256]
    solution_ref[...] = moved[:, 0:128]
    residual_ref[...] = residual
    both = precise(step_turned, sums)
    cross = both[:, 0:RHS]
    square = precise(shift(both, -RHS)[:, 0:RHS], step_matrix)
    norm_new = first[:, 0:RHS] - cross - cross.T + square
    ratio_turned = precise(norm_new, first_inverse)
    direction_ref[...] = residual + precise(ratio_turned, goals)

    for i, step in enumerate(OFFSETS):
        if step in DIRECT:
            landed(near_far.at[0], in_send.at[i])
        landed(near_far.at[0], across_send.at[i])
    for n in range(len(forwards)):
        landed(near_far.at[0], forward_send.at[n])
    for k in range(1, PLANE):
        landed(own, out_send.at[k])
        landed(outbox.at[0], box_send.at[k - 1])
    first_sum.sent()
    last_sum.sent()


def per_device(points, lengthscales, noise, targets):
    vmem = pl.BlockSpec(memory_space=pltpu.VMEM)
    out = jax.ShapeDtypeStruct((RHS, BLOCK), jnp.float32)
    dma = pltpu.SemaphoreType.DMA
    sums = [
        pltpu.VMEM((3, 8, 128), jnp.float32),
        pltpu.VMEM((PLANE, 8, 128), jnp.float32),
        pltpu.VMEM((RING, 8, 128), jnp.float32),
        pltpu.VMEM((2, 8, 128), jnp.float32),
    ]
    sum_sems = [dma((2,)), dma((2,)), dma((PLANE,)), dma, dma((RING,)), dma]
    slots = 2 * len(OFFSETS)
    return pl.pallas_call(
        kernel,
        out_shape=(out, out, out),
        in_specs=[vmem] * 4,
        out_specs=(vmem,) * 3,
        scratch_shapes=[
            pltpu.VMEM((slots, BLOCK + RHS, BLOCK), jnp.bfloat16),
            pltpu.VMEM((slots * BLOCK, BLOCK), jnp.bfloat16),
            pltpu.VMEM((PLANE, BLOCK, BLOCK), jnp.bfloat16),
            pltpu.VMEM((PLANE * BLOCK, PAIR), jnp.bfloat16),
            pltpu.VMEM((BLOCK, BLOCK), jnp.bfloat16),
            pltpu.VMEM((PLANE // 2, RHS, PAIR), jnp.float32),
            pltpu.VMEM((PLANE, RHS, BLOCK), jnp.float32),
            pltpu.VMEM((PLANE, RHS, BLOCK), jnp.float32),
            *sums,
            *sums,
            dma((len(OFFSETS),)),
            dma((len(OFFSETS),)),
            dma((len(OFFSETS),)),
            dma((len(OFFSETS),)),
            dma((16,)),
            dma((PLANE,)),
            dma((PLANE,)),
            dma((PLANE,)),
            dma,
            *sum_sems,
            *sum_sems,
        ],
        compiler_params=pltpu.CompilerParams(collective_id=0, has_side_effects=True, vmem_limit_bytes=48 << 20),
        cost_estimate=pl.CostEstimate(flops=3 << 30, bytes_accessed=1 << 20, transcendentals=1 << 24),
        name="step",
    )(points, lengthscales[None, :], noise[None, :], targets)


def solution(mesh):
    spread = P(None, ("row", "col"))
    return jax.shard_map(
        per_device,
        mesh=mesh,
        in_specs=(P(("row", "col"), None), P(), P(("row", "col")), spread),
        out_specs=(spread, spread, spread),
        check_vma=False,
    )
```

time: 396 us -> 80.5 us (0.20)
  blocking collectives: 271 us -> 0 us
  Pallas kernels: 0 us -> 75.6 us
  waiting for transfers between devices: 63.4 us -> 0 us
  matrix products: 27.5 us -> 0 us
  other arithmetic: 17.8 us -> 0 us
  between operations: 14.2 us -> 0.66 us
    psum x2 -> x0, blocking collectives: 213 us -> none  [the longest x1 113 us: per_device(): first = lax.psum(gram(targets, targets), ('row', 'col'))]
    pallas_call x0 -> x1, Pallas kernels: none -> 75.6 us  [per_device(): pl.pallas_call(kernel, out_shape=(out, out, out), in_specs=[vmem] * 4, ou...]
    all_gather x2 -> x0, blocking collectives: 57.6 us -> none  [the longest x1 29.3 us: per_device(): local_rows = lax.all_gather(scaled, 'col', axis=0, tiled=True)]
    reduce_scatter x1 -> x0, waiting for transfers between devices: 56.3 us -> none  [per_device(): lax.psum_scatter(partial_sum, 'col', scatter_dimension=1, tiled=True)]
    dot_general x10 -> x0, matrix products: 26.8 us -> none  [the longest x4 23 us: advance(): lax.dot_general(far_dirs, tile, (((0,), (1,)), ((), ())), preferred_eleme...]
    another operation x10 -> x0, other arithmetic: 13.4 us -> none  [chol_solve(): return jax.scipy.linalg.cho_solve((jnp.linalg.cholesky(matrix), True), rhs)]
    all_gather x1 -> x0, waiting for transfers between devices: 7.13 us -> none  [per_device(): lax.all_gather(scaled, 'row', axis=0, tiled=True)]
  transfers between devices with their start and end apart: 2 -> 0, of which waited for: 2 -> 0; matrix products, arithmetic and copies ran while one was open for 0% -> 0% of each run, Pallas kernels for 0% -> 0%
where the time goes in v1:
time: 80.5 us; the launch traced here: 80.3 us
  Pallas kernels  75.6 us (94%)
  local copies, waits for them, and re-layouts  4.03 us (5%)
    pallas_call x1, Pallas kernels, per_device(): pl.pallas_call(kernel, out_shape=(out, out, out), in_specs=[vmem] * 4, ou...  75.6 us
    unnamed x11, local copies, waits for them, and re-layouts  4.03 us

profile of v1, /device:TPU:1, one launch (start us, length us, event | category | flops | bytes accessed | tf_op | source)
XLA Modules:
  0.0 80.3 jit_solution(6907292169539827489)
XLA Ops:
  0.6 0.0 copy-start.2
  0.6 0.0 copy-start.3
  0.7 0.6 copy-done.2
  1.3 0.0 copy-done.3
  1.3 0.0 copy-start
  1.3 0.8 %copy-done = f32[128,128]{1,0:T(8,128)S(1)} copy-done((f32[128,128]{1,0:T(8,128)S(1)}, f32[128,128]{1,0:T(8,128)}, u32[]{:S(2)}) %copy-start) | copy-done | bytes 65560
  2.1 0.0 copy-start.1
  2.1 0.7 copy-done.1
  2.9 75.6 %step.1 = (f32[32,128]{1,0:T(8,128)S(1)}, f32[32,128]{1,0:T(8,128)S(1)}, f32[32,128]{1,0:T(8,128)S(1)}) custom-call(f32[128,128]{1,0:T(8,128)S(1)} %copy-done, f32[1,128]{1,0:T(1,128)S(1)} %bitcast.2, f32[1,128]{1,0:T(1,128)S(1)} %bitcast.3, f32[32,128]{1,0:T(8,128)S(1)} %copy-done.1), custom_call_target="tpu_custom_call" | custom-call | flops 3221225472 | bytes 1048576 | tf_op jit(solution)/shard_map/step/pallas_call | solution.py:360
  78.5 0.6 copy.10
  79.1 0.6 copy.11
  79.7 0.6 copy.12
Async XLA Ops:
  0.6 0.7 copy-start.2
  0.6 0.7 copy-start.3
  1.3 0.8 %copy-start = (f32[128,128]{1,0:T(8,128)S(1)}, f32[128,128]{1,0:T(8,128)}, u32[]{:S(2)}) copy-start(f32[128,128]{1,0:T(8,128)} %points.1) | copy-start | bytes 196612
  2.1 0.7 copy-start.1

commit v2 on v1

--- a/solution.py
+++ b/solution.py
@@ -16,12 +16,14 @@
 RING = 16
 BLOCK = 128
 RHS = 32
-DIRECT = (6, -6, 3, -3, 1, -1)
-NEAR = (0,) + DIRECT
-FAR = (2, -2, 4, -4, 5, -5, 7, -7, 8)
-OFFSETS = NEAR + FAR
-FORWARD = {6: (1, -1, 2), -6: (1, -1), 3: (1, -1), -3: (1, -1), 1: (), -1: ()}
+DIRECT = (3, -3, 1, -1)
+NEAR = (0, 1, -1, 3, -3)
+MIDDLE = (2, -2, 4, -4, 6, -6)
+FAR = (5, -5, 7, -7, 8)
+OFFSETS = NEAR + MIDDLE + FAR
+FORWARD = {3: (3, 1, -1), -3: (-3, -1, 1), 6: (2, 1, -1), -6: (-1, 1)}
 PAIR = 2 * BLOCK
+PAIRS = PLANE // 2
 
 
 def place():
@@ -86,19 +88,27 @@
     return (((5.0 / 3.0 * dist_sq + 1.0) + root_five * dist) * decay).astype(jnp.bfloat16)
 
 
-def product(dirs, rows, norms, out_points):
-    dist_sq = lax.dot_general(
+def distances(rows, norms, out_points):
+    return lax.dot_general(
         jnp.concatenate([rows, norms], axis=1), out_points, (((1,), (1,)), ((), ())), preferred_element_type=jnp.float32
     )
-    return jnp.dot(dirs, matern(dist_sq), preferred_element_type=jnp.float32)
 
 
 def eliminate(matrix):
-    row = lax.broadcasted_iota(jnp.int32, matrix.shape, 0)
-    for k in range(RHS):
-        pivot = matrix[k : k + 1, :] / matrix[k : k + 1, k : k + 1]
-        matrix = jnp.where(row == k, pivot, matrix - matrix[:, k : k + 1] * pivot)
-    return matrix
+    parts = [matrix[8 * i : 8 * i + 8] for i in range(RHS // 8)]
+    row = lax.broadcasted_iota(jnp.int32, parts[0].shape, 0)
+    for k in range(0, RHS, 2):
+        q, r = k // 8, k % 8
+        left = [jnp.broadcast_to(part[:, k : k + 1], part.shape) for part in parts]
+        right = [jnp.broadcast_to(part[:, k + 1 : k + 2], part.shape) for part in parts]
+        upper, lower = parts[q][r : r + 1], parts[q][r + 1 : r + 2]
+        a, b = left[q][r : r + 1], right[q][r : r + 1]
+        c, d = left[q][r + 1 : r + 2], right[q][r + 1 : r + 2]
+        scale = 1.0 / (a * d - b * c)
+        upper, lower = (d * upper - b * lower) * scale, (a * lower - c * upper) * scale
+        parts = [part - x * upper - y * lower for part, x, y in zip(parts, left, right)]
+        parts[q] = jnp.where(row == r, upper, jnp.where(row == r + 1, lower, parts[q]))
+    return jnp.concatenate(parts, axis=0)
 
 
 def shift(value, lanes):
@@ -175,12 +185,18 @@
 
 
 def kernel(
-    points, scales, noise, targets, solution_ref, residual_ref, direction_ref,
-    near_far, norms, out_raw, out_points, own, total, outbox, inbox,
+    points_in, scales_in, noise_in, targets_in, out_ref,
+    points, scales, noise, targets, dist_sq, near_far, norms, out_raw, out_points, own, total, outbox, inbox,
     parts_a, plane_a, ring_a, halves_a, parts_b, plane_b, ring_b, halves_b,
-    in_send, in_recv, across_send, across_recv, forward_send, out_send, out_recv, box_send, box_recv,
+    loaded, in_send, in_recv, across_send, across_recv, forward_send, out_send, out_recv, box_send, box_recv,
     cs_a, cr_a, ps_a, pr_a, rs_a, rr_a, cs_b, cr_b, ps_b, pr_b, rs_b, rr_b,
 ):
+    loads = [
+        pltpu.make_async_copy(src, dst, loaded.at[n])
+        for n, (src, dst) in enumerate(((points_in, points), (scales_in, scales), (noise_in, noise), (targets_in, targets)))
+    ]
+    for load in loads:
+        load.start()
     barrier = pltpu.get_barrier_semaphore()
 
     def greet(device):
@@ -195,6 +211,8 @@
     lax.fori_loop(1, PLANE, greet_plane, 0, unroll=True)
     greet(other_core())
 
+    for load in loads:
+        load.wait()
     goals = targets[...]
     scaled = (points[...] / scales[...]).astype(jnp.bfloat16)
     own[...] = scaled
@@ -209,21 +227,21 @@
 
     pl.semaphore_wait(barrier, (RING - 1) + (PLANE - 1) + 1)
 
-    for i, step in enumerate(OFFSETS):
-        if step in DIRECT:
-            remote(near_far.at[0], near_far.at[2 * i], in_send.at[i], in_recv.at[i], along_z(step)).start()
+    for step in DIRECT:
+        i = OFFSETS.index(step)
+        remote(near_far.at[0], near_far.at[2 * i], in_send.at[i], in_recv.at[i], along_z(step)).start()
 
     def across(i):
         remote(near_far.at[2 * i], near_far.at[2 * i + 1], across_send.at[i], across_recv.at[i], other_core()).start()
 
-    def send_out(k, _):
-        slot = 15 - back(k)
+    def send_out(n, _):
+        k, slot = back(n), 15 - n
         remote(own, out_raw.at[slot], out_send.at[k], out_recv.at[slot], in_plane(k)).start()
         return 0
 
+    first_sum.begin(first_part)
     lax.fori_loop(1, PLANE, send_out, 0, unroll=True)
     across(0)
-    first_sum.begin(first_part)
 
     def arrived(i):
         landed(near_far.at[2 * i], in_recv.at[i])
@@ -233,74 +251,112 @@
         norms[slot * BLOCK : (slot + 1) * BLOCK] = norm_lanes(near_far[slot, 0:BLOCK], 0)
 
     forwards = []
-    for step in (1, -1, 3, -3, 6, -6):
+
+    def pass_on(step):
         i = OFFSETS.index(step)
-        arrived(i)
-        for more in FORWARD[step]:
+        for more in FORWARD.get(step, ()):
             j = OFFSETS.index(step + more)
             n = len(forwards)
             forwards.append(j)
             remote(near_far.at[2 * i], near_far.at[2 * j], forward_send.at[n], in_recv.at[j], along_z(more)).start()
         take(2 * i)
-    first_sum.over_plane()
-
-    def take_out(slot, _):
+
+    def take_across(steps):
+        for step in steps:
+            i = OFFSETS.index(step)
+            landed(near_far.at[2 * i + 1], across_recv.at[i])
+            take(2 * i + 1)
+
+    def take_out(slot):
         landed(out_raw.at[slot], out_recv.at[slot])
         rows = out_raw[slot]
         at = pl.ds(pl.multiple_of(slot * BLOCK, BLOCK), BLOCK)
         out_points[at, 0:BLOCK] = rows * -2.0
         out_points[at, BLOCK:PAIR] = norm_lanes(rows, 3)
-        return 0
-
-    lax.fori_loop(0, PLANE - 1, take_out, 0)
-
-    def take_across(i):
-        landed(near_far.at[2 * i + 1], across_recv.at[i])
-        take(2 * i + 1)
-
-    for i in range(len(NEAR)):
-        take_across(i)
-
-    def partial(begin, end, o):
-        rows = near_far[begin:end, 0:BLOCK].reshape((end - begin) * BLOCK, BLOCK)
-        dirs = jnp.concatenate([near_far[s, BLOCK : BLOCK + RHS] for s in range(begin, end)], axis=1)
-        at = pl.ds(pl.multiple_of(o * PAIR, PAIR), PAIR)
-        return product(dirs, rows, norms[begin * BLOCK : end * BLOCK], out_points[at, :])
-
-    near_slots, slots = 2 * len(NEAR), 2 * len(OFFSETS)
-
-    def near_part(o, _):
-        total[o] = partial(0, near_slots, o)
-        return 0
-
-    lax.fori_loop(0, PLANE // 2, near_part, 0)
-
-    for i in range(len(NEAR), len(OFFSETS)):
-        arrived(i)
-        take(2 * i)
-    first_sum.over_ring()
-    for i in range(len(NEAR), len(OFFSETS)):
-        take_across(i)
-
-    def far_part(o, _):
-        value = total[o] + partial(near_slots, slots, o)
+
+    def take_pair(o):
+        take_out(2 * o)
+
+        @pl.when(o < PAIRS - 1)
+        def _():
+            take_out(2 * o + 1)
+
+    def sweep(steps, begin, end, finish, order, prepare=None):
+        low = 2 * OFFSETS.index(steps[0])
+        high = low + 2 * len(steps)
+        size = (high - low) * BLOCK
+
+        def ahead(o):
+            rows = near_far[low:high, 0:BLOCK].reshape(size, BLOCK)
+            at = pl.ds(pl.multiple_of(o * PAIR, PAIR), PAIR)
+            return distances(rows, norms[low * BLOCK : high * BLOCK], out_points[at, :])
+
+        def one(n, slot):
+            o, later = order(n), order(jnp.minimum(n + 1, PAIRS - 1))
+            if prepare is not None:
+                pl.when(n < PAIRS - 1)(lambda: prepare(later))
+            following = ahead(later)
+            dirs = jnp.concatenate([near_far[s, BLOCK : BLOCK + RHS] for s in range(low, high)], axis=1)
+            value = jnp.dot(dirs, matern(dist_sq[slot, 0:size]), preferred_element_type=jnp.float32)
+            dist_sq[1 - slot, 0:size] = following
+            finish(o, value)
+
+        def two(h, _):
+            one(2 * h, 0)
+            one(2 * h + 1, 1)
+            return 0
+
+        if begin == 0:
+            if prepare is not None:
+                prepare(order(0))
+            dist_sq[0, 0:size] = ahead(order(0))
+        lax.fori_loop(begin // 2, end // 2, two, 0)
+
+    def start_total(o, value):
+        total[o] = value
+
+    def add_total(o, value):
+        total[o] += value
+
+    def post(o, value):
+        value = total[o] + value
         outbox[2 * o] = value[:, 0:BLOCK]
         outbox[2 * o + 1] = value[:, BLOCK:PAIR]
 
-        def post(slot):
-            step = 15 - slot
-            remote(outbox.at[slot], inbox.at[slot], box_send.at[slot], box_recv, in_plane(step)).start()
-
-        post(2 * o)
-
-        @pl.when(o < PLANE // 2 - 1)
+        def send(slot):
+            remote(outbox.at[slot], inbox.at[slot], box_send.at[slot], box_recv, in_plane(15 - slot)).start()
+
+        send(2 * o)
+
+        @pl.when(o < PAIRS - 1)
         def _():
-            post(2 * o + 1)
-
-        return 0
-
-    lax.fori_loop(0, PLANE // 2, far_part, 0)
+            send(2 * o + 1)
+
+    def up(n):
+        return n
+
+    def down(n):
+        return PAIRS - 1 - n
+
+    def receive(steps):
+        for step in steps:
+            arrived(OFFSETS.index(step))
+            pass_on(step)
+
+    first_sum.over_plane()
+    receive((3, -3, 1, -1))
+    take_across(NEAR)
+    sweep(NEAR, 0, 6, start_total, down, take_pair)
+    receive((2, -2, 4, -4))
+    first_sum.over_ring()
+    sweep(NEAR, 6, PAIRS, start_total, down, take_pair)
+    receive((6, -6))
+    take_across(MIDDLE)
+    sweep(MIDDLE, 0, PAIRS, add_total, up)
     first_sum.over_cores()
+    receive(FAR)
+    take_across(FAR)
+    sweep(FAR, 0, PAIRS, post, up)
 
     lane = lax.broadcasted_iota(jnp.int32, (RHS, 128), 1)
     row = lax.broadcasted_iota(jnp.int32, (RHS, 128), 0)
@@ -323,14 +379,14 @@
     step_turned = step_matrix.T
     moved = precise(step_turned, jnp.concatenate([goals, image], axis=1))
     residual = goals - moved[:, 128:256]
-    solution_ref[...] = moved[:, 0:128]
-    residual_ref[...] = residual
+    out_ref[0] = moved[:, 0:128]
+    out_ref[1] = residual
     both = precise(step_turned, sums)
     cross = both[:, 0:RHS]
     square = precise(shift(both, -RHS)[:, 0:RHS], step_matrix)
     norm_new = first[:, 0:RHS] - cross - cross.T + square
     ratio_turned = precise(norm_new, first_inverse)
-    direction_ref[...] = residual + precise(ratio_turned, goals)
+    out_ref[2] = residual + precise(ratio_turned, goals)
 
     for i, step in enumerate(OFFSETS):
         if step in DIRECT:
@@ -346,8 +402,6 @@
 
 
 def per_device(points, lengthscales, noise, targets):
-    vmem = pl.BlockSpec(memory_space=pltpu.VMEM)
-    out = jax.ShapeDtypeStruct((RHS, BLOCK), jnp.float32)
     dma = pltpu.SemaphoreType.DMA
     sums = [
         pltpu.VMEM((3, 8, 128), jnp.float32),
@@ -357,22 +411,28 @@
     ]
     sum_sems = [dma((2,)), dma((2,)), dma((PLANE,)), dma, dma((RING,)), dma]
     slots = 2 * len(OFFSETS)
-    return pl.pallas_call(
+    outs = pl.pallas_call(
         kernel,
-        out_shape=(out, out, out),
-        in_specs=[vmem] * 4,
-        out_specs=(vmem,) * 3,
+        out_shape=jax.ShapeDtypeStruct((3, RHS, BLOCK), jnp.float32),
+        in_specs=[pl.BlockSpec(memory_space=pltpu.HBM)] * 4,
+        out_specs=pl.BlockSpec(memory_space=pltpu.VMEM),
         scratch_shapes=[
+            pltpu.VMEM((BLOCK, BLOCK), jnp.float32),
+            pltpu.VMEM((1, BLOCK), jnp.float32),
+            pltpu.VMEM((1, BLOCK), jnp.float32),
+            pltpu.VMEM((RHS, BLOCK), jnp.float32),
+            pltpu.VMEM((2, 2 * len(MIDDLE) * BLOCK, PAIR), jnp.float32),
             pltpu.VMEM((slots, BLOCK + RHS, BLOCK), jnp.bfloat16),
             pltpu.VMEM((slots * BLOCK, BLOCK), jnp.bfloat16),
             pltpu.VMEM((PLANE, BLOCK, BLOCK), jnp.bfloat16),
             pltpu.VMEM((PLANE * BLOCK, PAIR), jnp.bfloat16),
             pltpu.VMEM((BLOCK, BLOCK), jnp.bfloat16),
-            pltpu.VMEM((PLANE // 2, RHS, PAIR), jnp.float32),
+            pltpu.VMEM((PAIRS, RHS, PAIR), jnp.float32),
             pltpu.VMEM((PLANE, RHS, BLOCK), jnp.float32),
             pltpu.VMEM((PLANE, RHS, BLOCK), jnp.float32),
             *sums,
             *sums,
+            dma((4,)),
             dma((len(OFFSETS),)),
             dma((len(OFFSETS),)),
             dma((len(OFFSETS),)),
@@ -385,10 +445,11 @@
             *sum_sems,
             *sum_sems,
         ],
-        compiler_params=pltpu.CompilerParams(collective_id=0, has_side_effects=True, vmem_limit_bytes=48 << 20),
+        compiler_params=pltpu.CompilerParams(collective_id=0, has_side_effects=True, vmem_limit_bytes=60 << 20),
         cost_estimate=pl.CostEstimate(flops=3 << 30, bytes_accessed=1 << 20, transcendentals=1 << 24),
         name="step",
     )(points, lengthscales[None, :], noise[None, :], targets)
+    return outs[0], outs[1], outs[2]
 
 
 def solution(mesh):

time: 80.5 us -> 70.2 us (0.87)
  Pallas kernels: 75.6 us -> 68 us
  local copies, waits for them, and re-layouts: 4.03 us -> 1.37 us
    pallas_call x1, Pallas kernels: 75.6 us -> 68 us  [per_device(): pl.pallas_call(kernel, out_shape=jax.ShapeDtypeStruct((3, RHS, BLOCK), jn...]
    unnamed x11 -> x0, local copies, waits for them, and re-layouts: 4.03 us -> none
    squeeze x0 -> x1, local copies, waits for them, and re-layouts: none -> 1.37 us  [per_device(): return (outs[0], outs[1], outs[2])]
where the time goes in v2:
time: 70.2 us; the launch traced here: 70 us
  Pallas kernels  68 us (97%)
  local copies, waits for them, and re-layouts  1.37 us (2%)
    pallas_call x1, Pallas kernels, per_device(): pl.pallas_call(kernel, out_shape=jax.ShapeDtypeStruct((3, RHS, BLOCK), jn...  68 us

profile of v2, /device:TPU:1, one launch (start us, length us, event | category | flops | bytes accessed | tf_op | source)
XLA Modules:
  0.0 70.0 jit_solution(2955492592830362671)
XLA Ops:
  0.6 68.0 %step.1 = f32[3,32,128]{2,1,0:T(8,128)} custom-call(f32[128,128]{1,0:T(8,128)} %points_in.1, f32[1,128]{1,0:T(1,128)} %bitcast.8, f32[1,128]{1,0:T(1,128)} %bitcast.9, f32[32,128]{1,0:T(8,128)} %targets_in.1), custom_call_target="tpu_custom_call" | custom-call | flops 3221225472 | bytes 1048576 | tf_op jit(solution)/shard_map/step/pallas_call | solution.py:414
  68.6 1.4 %slice_bitcast_fusion = (f32[32,128]{1,0:T(8,128)}, f32[32,128]{1,0:T(8,128)}, f32[32,128]{1,0:T(8,128)}) fusion(f32[3,32,128]{2,1,0:T(8,128)} %step.1), kind=kLoop, calls=%fused_computation | loop fusion | bytes 98304 | tf_op jit(solution)/shard_map/squeeze | solution.py:452

commit v3 on v2

--- a/solution.py
+++ b/solution.py
@@ -152,7 +152,7 @@
         self.plane[me] = self.parts[0] + self.parts[2]
 
         def send(k, _):
-            remote(self.plane.at[me], self.plane.at[me], self.plane_send.at[k], self.plane_recv, in_plane(k)).start()
+            remote(self.plane.at[me], self.plane.at[me], self.plane_send, self.plane_recv, in_plane(k)).start()
             return 0
 
         lax.fori_loop(1, PLANE, send, 0, unroll=True)
@@ -162,7 +162,7 @@
         landed(self.plane.at[pl.ds(1, PLANE - 1)], self.plane_recv)
         self.ring[me] = jnp.sum(self.plane[...], axis=0)
         for k in (8, -7, 7, -6, 6, -5, 5, -4, 4, -3, 3, -2, 2, -1, 1):
-            remote(self.ring.at[me], self.ring.at[me], self.ring_send.at[k % RING], self.ring_recv, along_z(k)).start()
+            remote(self.ring.at[me], self.ring.at[me], self.ring_send, self.ring_recv, along_z(k)).start()
 
     def over_cores(self):
         core = place()[2]
@@ -178,17 +178,15 @@
     def sent(self):
         landed(self.parts.at[1], self.core_send.at[0])
         landed(self.halves.at[0], self.core_send.at[1])
-        for k in range(1, PLANE):
-            landed(self.plane.at[0], self.plane_send.at[k])
-        for k in range(1, RING):
-            landed(self.ring.at[0], self.ring_send.at[k])
+        landed(self.plane.at[pl.ds(1, PLANE - 1)], self.plane_send)
+        landed(self.ring.at[pl.ds(1, RING - 1)], self.ring_send)
 
 
 def kernel(
     points_in, scales_in, noise_in, targets_in, out_ref,
     points, scales, noise, targets, dist_sq, near_far, norms, out_raw, out_points, own, total, outbox, inbox,
     parts_a, plane_a, ring_a, halves_a, parts_b, plane_b, ring_b, halves_b,
-    loaded, in_send, in_recv, across_send, across_recv, forward_send, out_send, out_recv, box_send, box_recv,
+    loaded, in_send, in_recv, across_send, across_recv, out_send, out_recv, box_send, box_recv,
     cs_a, cr_a, ps_a, pr_a, rs_a, rr_a, cs_b, cr_b, ps_b, pr_b, rs_b, rr_b,
 ):
     loads = [
@@ -229,14 +227,14 @@
 
     for step in DIRECT:
         i = OFFSETS.index(step)
-        remote(near_far.at[0], near_far.at[2 * i], in_send.at[i], in_recv.at[i], along_z(step)).start()
+        remote(near_far.at[0], near_far.at[2 * i], in_send, in_recv.at[i], along_z(step)).start()
 
     def across(i):
-        remote(near_far.at[2 * i], near_far.at[2 * i + 1], across_send.at[i], across_recv.at[i], other_core()).start()
+        remote(near_far.at[2 * i], near_far.at[2 * i + 1], across_send, across_recv.at[i], other_core()).start()
 
     def send_out(n, _):
         k, slot = back(n), 15 - n
-        remote(own, out_raw.at[slot], out_send.at[k], out_recv.at[slot], in_plane(k)).start()
+        remote(own, out_raw.at[slot], out_send, out_recv.at[slot], in_plane(k)).start()
         return 0
 
     first_sum.begin(first_part)
@@ -249,16 +247,12 @@
 
     def take(slot):
         norms[slot * BLOCK : (slot + 1) * BLOCK] = norm_lanes(near_far[slot, 0:BLOCK], 0)
-
-    forwards = []
 
     def pass_on(step):
         i = OFFSETS.index(step)
         for more in FORWARD.get(step, ()):
             j = OFFSETS.index(step + more)
-            n = len(forwards)
-            forwards.append(j)
-            remote(near_far.at[2 * i], near_far.at[2 * j], forward_send.at[n], in_recv.at[j], along_z(more)).start()
+            remote(near_far.at[2 * i], near_far.at[2 * j], in_send, in_recv.at[j], along_z(more)).start()
         take(2 * i)
 
     def take_across(steps):
@@ -324,7 +318,7 @@
         outbox[2 * o + 1] = value[:, BLOCK:PAIR]
 
         def send(slot):
-            remote(outbox.at[slot], inbox.at[slot], box_send.at[slot], box_recv, in_plane(15 - slot)).start()
+            remote(outbox.at[slot], inbox.at[slot], box_send, box_recv, in_plane(15 - slot)).start()
 
         send(2 * o)
 
@@ -346,11 +340,12 @@
     first_sum.over_plane()
     receive((3, -3, 1, -1))
     take_across(NEAR)
-    sweep(NEAR, 0, 6, start_total, down, take_pair)
+    sweep(NEAR, 0, 4, start_total, down, take_pair)
     receive((2, -2, 4, -4))
     first_sum.over_ring()
+    sweep(NEAR, 4, 6, start_total, down, take_pair)
+    receive((6, -6))
     sweep(NEAR, 6, PAIRS, start_total, down, take_pair)
-    receive((6, -6))
     take_across(MIDDLE)
     sweep(MIDDLE, 0, PAIRS, add_total, up)
     first_sum.over_cores()
@@ -388,15 +383,10 @@
     ratio_turned = precise(norm_new, first_inverse)
     out_ref[2] = residual + precise(ratio_turned, goals)
 
-    for i, step in enumerate(OFFSETS):
-        if step in DIRECT:
-            landed(near_far.at[0], in_send.at[i])
-        landed(near_far.at[0], across_send.at[i])
-    for n in range(len(forwards)):
-        landed(near_far.at[0], forward_send.at[n])
-    for k in range(1, PLANE):
-        landed(own, out_send.at[k])
-        landed(outbox.at[0], box_send.at[k - 1])
+    landed(near_far.at[pl.ds(0, len(OFFSETS) - 1)], in_send)
+    landed(near_far.at[pl.ds(0, len(OFFSETS))], across_send)
+    landed(out_raw.at[pl.ds(0, PLANE - 1)], out_send)
+    landed(outbox.at[pl.ds(0, PLANE - 1)], box_send)
     first_sum.sent()
     last_sum.sent()
 
@@ -409,7 +399,7 @@
         pltpu.VMEM((RING, 8, 128), jnp.float32),
         pltpu.VMEM((2, 8, 128), jnp.float32),
     ]
-    sum_sems = [dma((2,)), dma((2,)), dma((PLANE,)), dma, dma((RING,)), dma]
+    sum_sems = [dma((2,)), dma((2,)), dma, dma, dma, dma]
     slots = 2 * len(OFFSETS)
     outs = pl.pallas_call(
         kernel,
@@ -433,14 +423,13 @@
             *sums,
             *sums,
             dma((4,)),
+            dma,
             dma((len(OFFSETS),)),
+            dma,
             dma((len(OFFSETS),)),
-            dma((len(OFFSETS),)),
-            dma((len(OFFSETS),)),
-            dma((16,)),
+            dma,
             dma((PLANE,)),
-            dma((PLANE,)),
-            dma((PLANE,)),
+            dma,
             dma,
             *sum_sems,
             *sum_sems,

time: 70.2 us -> 67.9 us (0.967)
  Pallas kernels: 68 us -> 65.7 us
    pallas_call x1, Pallas kernels: 68 us -> 65.7 us  [per_device(): pl.pallas_call(kernel, out_shape=jax.ShapeDtypeStruct((3, RHS, BLOCK), jn...]
where the time goes in v3:
time: 67.9 us; the launch traced here: 67.7 us
  Pallas kernels  65.7 us (97%)
  local copies, waits for them, and re-layouts  1.37 us (2%)
    pallas_call x1, Pallas kernels, per_device(): pl.pallas_call(kernel, out_shape=jax.ShapeDtypeStruct((3, RHS, BLOCK), jn...  65.7 us
    squeeze x1, local copies, waits for them, and re-layouts, per_device(): return (outs[0], outs[1], outs[2])  1.37 us

profile of v3, /device:TPU:1, one launch (start us, length us, event | category | flops | bytes accessed | tf_op | source)
XLA Modules:
  0.0 67.7 jit_solution(16434561175304980148)
XLA Ops:
  0.6 65.7 %step.1 = f32[3,32,128]{2,1,0:T(8,128)} custom-call(f32[128,128]{1,0:T(8,128)} %points_in.1, f32[1,128]{1,0:T(1,128)} %bitcast.8, f32[1,128]{1,0:T(1,128)} %bitcast.9, f32[32,128]{1,0:T(8,128)} %targets_in.1), custom_call_target="tpu_custom_call" | custom-call | flops 3221225472 | bytes 1048576 | tf_op jit(solution)/shard_map/step/pallas_call | solution.py:404
  66.3 1.4 %slice_bitcast_fusion = (f32[32,128]{1,0:T(8,128)}, f32[32,128]{1,0:T(8,128)}, f32[32,128]{1,0:T(8,128)}) fusion(f32[3,32,128]{2,1,0:T(8,128)} %step.1), kind=kLoop, calls=%fused_computation | loop fusion | bytes 98304 | tf_op jit(solution)/shard_map/squeeze | solution.py:441

commit v4 on v3

--- a/solution.py
+++ b/solution.py
@@ -237,9 +237,9 @@
         remote(own, out_raw.at[slot], out_send, out_recv.at[slot], in_plane(k)).start()
         return 0
 
-    first_sum.begin(first_part)
     lax.fori_loop(1, PLANE, send_out, 0, unroll=True)
     across(0)
+    first_sum.begin(first_part)
 
     def arrived(i):
         landed(near_far.at[2 * i], in_recv.at[i])
@@ -275,7 +275,7 @@
         def _():
             take_out(2 * o + 1)
 
-    def sweep(steps, begin, end, finish, order, prepare=None):
+    def sweep(steps, finish, order, prepare=None, between=()):
         low = 2 * OFFSETS.index(steps[0])
         high = low + 2 * len(steps)
         size = (high - low) * BLOCK
@@ -296,15 +296,16 @@
             finish(o, value)
 
         def two(h, _):
+            for at in between:
+                pl.when(h == at)(between[at])
             one(2 * h, 0)
             one(2 * h + 1, 1)
             return 0
 
-        if begin == 0:
-            if prepare is not None:
-                prepare(order(0))
-            dist_sq[0, 0:size] = ahead(order(0))
-        lax.fori_loop(begin // 2, end // 2, two, 0)
+        if prepare is not None:
+            prepare(order(0))
+        dist_sq[0, 0:size] = ahead(order(0))
+        lax.fori_loop(0, PAIRS // 2, two, 0)
 
     def start_total(o, value):
         total[o] = value
@@ -337,21 +338,23 @@
             arrived(OFFSETS.index(step))
             pass_on(step)
 
+    receive((3, -3, 1, -1))
     first_sum.over_plane()
-    receive((3, -3, 1, -1))
     take_across(NEAR)
-    sweep(NEAR, 0, 4, start_total, down, take_pair)
-    receive((2, -2, 4, -4))
-    first_sum.over_ring()
-    sweep(NEAR, 4, 6, start_total, down, take_pair)
-    receive((6, -6))
-    sweep(NEAR, 6, PAIRS, start_total, down, take_pair)
+    def after_four():
+        receive((2, -2, 4, -4))
+        first_sum.over_ring()
+
+    def after_six():
+        receive((6, -6))
+
+    sweep(NEAR, start_total, down, take_pair, {2: after_four, 3: after_six})
     take_across(MIDDLE)
-    sweep(MIDDLE, 0, PAIRS, add_total, up)
+    sweep(MIDDLE, add_total, up)
     first_sum.over_cores()
     receive(FAR)
     take_across(FAR)
-    sweep(FAR, 0, PAIRS, post, up)
+    sweep(FAR, post, up)
 
     lane = lax.broadcasted_iota(jnp.int32, (RHS, 128), 1)
     row = lax.broadcasted_iota(jnp.int32, (RHS, 128), 0)
@@ -365,6 +368,7 @@
     last_sum.begin(wide(gram(image, jnp.concatenate([goals, image], axis=0))))
     last_sum.over_plane()
     last_sum.over_ring()
+    weighted = precise(first_inverse, goals)
     last_sum.over_cores()
     sums = last_sum.end()
     turned = sums[:, 0:RHS]
@@ -380,8 +384,7 @@
     cross = both[:, 0:RHS]
     square = precise(shift(both, -RHS)[:, 0:RHS], step_matrix)
     norm_new = first[:, 0:RHS] - cross - cross.T + square
-    ratio_turned = precise(norm_new, first_inverse)
-    out_ref[2] = residual + precise(ratio_turned, goals)
+    out_ref[2] = residual + precise(norm_new, weighted)
 
     landed(near_far.at[pl.ds(0, len(OFFSETS) - 1)], in_send)
     landed(near_far.at[pl.ds(0, len(OFFSETS))], across_send)

time: 67.9 us -> 67.6 us (level)
  no operation moved by 1% of the time
where the time goes in v4:
time: 67.6 us; the launch traced here: 67.3 us
  Pallas kernels  65.3 us (97%)
  local copies, waits for them, and re-layouts  1.37 us (2%)
    pallas_call x1, Pallas kernels, per_device(): pl.pallas_call(kernel, out_shape=jax.ShapeDtypeStruct((3, RHS, BLOCK), jn...  65.3 us
    squeeze x1, local copies, waits for them, and re-layouts, per_device(): return (outs[0], outs[1], outs[2])  1.37 us

profile of v4, /device:TPU:1, one launch (start us, length us, event | category | flops | bytes accessed | tf_op | source)
XLA Modules:
  0.0 67.3 jit_solution(5455080558425565276)
XLA Ops:
  0.6 65.3 %step.1 = f32[3,32,128]{2,1,0:T(8,128)} custom-call(f32[128,128]{1,0:T(8,128)} %points_in.1, f32[1,128]{1,0:T(1,128)} %bitcast.8, f32[1,128]{1,0:T(1,128)} %bitcast.9, f32[32,128]{1,0:T(8,128)} %targets_in.1), custom_call_target="tpu_custom_call" | custom-call | flops 3221225472 | bytes 1048576 | tf_op jit(solution)/shard_map/step/pallas_call | solution.py:407
  66.0 1.4 %slice_bitcast_fusion = (f32[32,128]{1,0:T(8,128)}, f32[32,128]{1,0:T(8,128)}, f32[32,128]{1,0:T(8,128)}) fusion(f32[3,32,128]{2,1,0:T(8,128)} %step.1), kind=kLoop, calls=%fused_computation | loop fusion | bytes 98304 | tf_op jit(solution)/shard_map/squeeze | solution.py:444
